TPU v7x, 32 devices: a whole 2x2x4 slice. The times are simulated.
32 devices in a mesh: energy: 8 (over y, x, core), dom: 4 (over z).
Axes of the slice: x: 2, y: 2, z: 4, core: 2. Of those that a mesh axis runs over, the one named last changes fastest.
Arguments:
- lesser_occupancy: float32 [8, 8, 128], P('energy', 'dom'), may hold values from 0.05 to 0.5
- greater_occupancy: float32 [8, 8, 128], P('energy', 'dom'), may hold values from 0.05 to 0.5
- hamiltonian: float32 [8, 2, 128, 128], P('dom'), as said below
- couplings: float32 [8, 2, 128, 128], P('dom')
- right_lead: float32 [2, 128, 128], replicated
- phonon_steps: int32 [6], replicated, may hold values from 1 to 4, as said below
- emission_strength: float32 [6], replicated, may hold values from 0.02 to 0.08
- absorption_strength: float32 [6], replicated, may hold values from 0.01 to 0.05
Outputs:
- green_diag: float32 [8, 8, 2, 128, 128], P('energy', 'dom')
- scattering_in: float32 [8, 8, 128], P('energy', 'dom')
- scattering_out: float32 [8, 8, 128], P('energy', 'dom')
Inputs may be any that keep to these rules, and one draw needn't show every extreme that they name: `phonon_steps`: each mode's step in energy indices; some mode's step is 4. `hamiltonian`: every block is Hermitian: its real plane is symmetric and its imaginary plane antisymmetric.
All inputs are finite; a program needn't handle non-finite values.
Results may differ from a plain program's by a relative error of at most 0.00026.
Values sent between devices are 32-bit elements; how exact they have to be, the bound alone decides.
A program may use at most 64 MiB of HBM per device.

v0:
```python
import jax
import jax.numpy as jnp
from jax import lax
from jax.sharding import PartitionSpec as P

MODES = 6
SMAX = 4


energy_low = -1.0
energy_span = 2.0
damping = 0.02


def passed_along(value, axis, by):
    peers = lax.axis_size(axis)
    pairs = [(i, i + by) for i in range(peers) if 0 <= i + by < peers]
    return lax.ppermute(value, axis, pairs)


def complex_product(left_factor, right_factor):
    highest = lax.Precision.HIGHEST
    left_real = left_factor[..., 0, :, :]
    left_imag = left_factor[..., 1, :, :]
    right_real = right_factor[..., 0, :, :]
    right_imag = right_factor[..., 1, :, :]
    real_part = jnp.matmul(left_real, right_real, precision=highest) - jnp.matmul(
        left_imag, right_imag, precision=highest
    )
    imag_part = jnp.matmul(left_real, right_imag, precision=highest) + jnp.matmul(
        left_imag, right_real, precision=highest
    )
    return jnp.stack([real_part, imag_part], axis=-3)


def adjoint(matrix):
    return jnp.stack(
        [jnp.swapaxes(matrix[..., 0, :, :], -1, -2), -jnp.swapaxes(matrix[..., 1, :, :], -1, -2)],
        axis=-3,
    )


def complex_identity(like_block):
    order_size = like_block.shape[-1]
    unit_matrix = jnp.eye(order_size, dtype=like_block.dtype)
    planes = jnp.stack([unit_matrix, jnp.zeros_like(unit_matrix)])
    return jnp.broadcast_to(planes, like_block.shape)


def times_half_i(matrix):
    return jnp.stack([-0.5 * matrix[..., 1, :, :], 0.5 * matrix[..., 0, :, :]], axis=-3)


def invert(matrix):
    highest = lax.Precision.HIGHEST
    order_size = matrix.shape[-1]
    real_part = matrix[..., 0, :, :]
    imag_part = matrix[..., 1, :, :]
    upper_half = jnp.concatenate([real_part, -imag_part], axis=-1)
    lower_half = jnp.concatenate([imag_part, real_part], axis=-1)
    embedded = jnp.concatenate([upper_half, lower_half], axis=-2)
    transposed = jnp.swapaxes(embedded, -1, -2)
    normal_matrix = jnp.matmul(transposed, embedded, precision=highest)
    factor = jnp.linalg.cholesky(normal_matrix)
    solved = jax.scipy.linalg.cho_solve((factor, True), transposed[..., :order_size])
    estimate = jnp.stack([solved[..., :order_size, :], solved[..., order_size:, :]], axis=-3)
    residue = 2.0 * complex_identity(estimate) - complex_product(matrix, estimate)
    return complex_product(estimate, residue)


def local(
    lesser_occupancy,
    greater_occupancy,
    hamiltonian,
    couplings,
    right_lead,
    phonon_steps,
    emission_strength,
    absorption_strength,
):
    energies_here = lesser_occupancy.shape[0]
    blocks_here = hamiltonian.shape[0]
    orbitals = hamiltonian.shape[-1]
    energy_count = lax.axis_size("energy")
    partitions = lax.axis_size("dom")
    energy_place = lax.axis_index("energy")
    dom_place = lax.axis_index("dom")
    stacked = jnp.stack([lesser_occupancy, greater_occupancy])
    reach_devices = -(-SMAX // energies_here)
    pieces = []
    for offset in range(reach_devices, -reach_devices - 1, -1):
        if offset == 0:
            pieces.append(stacked)
        else:
            pieces.append(passed_along(stacked, "energy", offset))
    window = jnp.concatenate(pieces, axis=1)
    base_start = reach_devices * energies_here
    scattering_in = jnp.zeros_like(lesser_occupancy)
    scattering_out = jnp.zeros_like(greater_occupancy)
    for mode_number in range(MODES):
        step_size = phonon_steps[mode_number]
        above_part = lax.dynamic_slice_in_dim(window, base_start + step_size, energies_here, 1)
        below_part = lax.dynamic_slice_in_dim(window, base_start - step_size, energies_here, 1)
        scattering_in = (
            scattering_in
            + emission_strength[mode_number] * above_part[0]
            + absorption_strength[mode_number] * below_part[0]
        )
        scattering_out = (
            scattering_out
            + emission_strength[mode_number] * below_part[1]
            + absorption_strength[mode_number] * above_part[1]
        )
    broadening = 0.5 * (scattering_in + scattering_out)
    energy_total = energies_here * energy_count
    positions = (energy_place * energies_here + jnp.arange(energies_here)).astype(jnp.float32)
    energy_values = energy_low + energy_span * (positions + 0.5) / energy_total
    unit_matrix = jnp.eye(orbitals, dtype=jnp.float32)
    system_list = []
    for number in range(blocks_here):
        real_part = energy_values[:, None, None] * unit_matrix - hamiltonian[number, 0]
        imag_part = (
            damping * unit_matrix
            - hamiltonian[number, 1]
            + unit_matrix * broadening[:, number, None, :]
        )
        system_list.append(jnp.stack([real_part, imag_part], axis=1))
    link_adjoints = [adjoint(couplings[number]) for number in range(blocks_here)]
    first_lead = times_half_i(complex_product(link_adjoints[0], couplings[0]))
    last_lead = times_half_i(complex_product(right_lead, adjoint(right_lead)))
    system_list[0] = system_list[0] + jnp.where(
        dom_place == 0, first_lead, jnp.zeros_like(first_lead)
    )
    system_list[blocks_here - 1] = system_list[blocks_here - 1] + jnp.where(
        dom_place == partitions - 1, last_lead, jnp.zeros_like(last_lead)
    )
    green_here = invert(system_list[0])
    head_tail = green_here
    tail_head = green_here
    head_block = green_here
    number = 1
    coupled = complex_product(complex_product(link_adjoints[number], green_here), couplings[number])
    green_here = invert(system_list[number] - coupled)
    bridge = complex_product(head_tail, couplings[number])
    head_tail = complex_product(bridge, green_here)
    returning = complex_product(link_adjoints[number], tail_head)
    tail_head = complex_product(green_here, returning)
    head_block = head_block + complex_product(head_tail, returning)
    edge_left = complex_product(complex_product(couplings[0], head_block), link_adjoints[0])
    edge_across = complex_product(couplings[0], head_tail)
    edge_return = complex_product(tail_head, link_adjoints[0])
    edge_right = green_here
    zero_block = jnp.zeros_like(edge_right)
    unit_block = complex_identity(zero_block)

    def extend_prefix(surface):
        mixing = complex_product(surface, edge_left)
        resolvent = invert(unit_block - mixing)
        carried = complex_product(resolvent, surface)
        return edge_right + complex_product(complex_product(edge_return, carried), edge_across)

    def extend_suffix(surface):
        mixing = complex_product(edge_right, surface)
        resolvent = invert(unit_block - mixing)
        inner_return = complex_product(resolvent, edge_return)
        through = complex_product(edge_across, surface)
        return edge_left + complex_product(through, inner_return)

    def silent(surface):
        return jnp.zeros_like(surface)

    def relay_turn(turn_number, relay_state):
        surface_left, self_right = relay_state
        sent_left = lax.cond(dom_place == turn_number, extend_prefix, silent, surface_left)
        sent_right = lax.cond(
            dom_place == partitions - 1 - turn_number, extend_suffix, silent, self_right
        )
        from_left = passed_along(sent_left, "dom", 1)
        from_right = passed_along(sent_right, "dom", -1)
        surface_left = jnp.where(dom_place == turn_number + 1, from_left, surface_left)
        self_right = jnp.where(dom_place == partitions - 2 - turn_number, from_right, self_right)
        return (surface_left, self_right)

    surface_left, self_right = lax.fori_loop(
        0, partitions - 1, relay_turn, (zero_block, zero_block)
    )
    left_self = complex_product(complex_product(link_adjoints[0], surface_left), couplings[0])
    system_list[0] = system_list[0] - left_self
    system_list[blocks_here - 1] = system_list[blocks_here - 1] - self_right
    left_greens = [invert(system_list[0])]
    number = 1
    coupled = complex_product(
        complex_product(link_adjoints[number], left_greens[-1]), couplings[number]
    )
    left_greens.append(invert(system_list[number] - coupled))
    diagonal = [left_greens[-1]]
    number = 0
    own_green = left_greens[number]
    carried = complex_product(complex_product(own_green, couplings[number + 1]), diagonal[0])
    diagonal.insert(
        0,
        own_green + complex_product(complex_product(carried, link_adjoints[number + 1]), own_green),
    )
    green_diag = jnp.stack(diagonal, axis=1)
    return (green_diag, scattering_in, scattering_out)


def solution(mesh):
    return jax.shard_map(
        local,
        mesh=mesh,
        in_specs=(
            P("energy", "dom", None),
            P("energy", "dom", None),
            P("dom", None, None, None),
            P("dom", None, None, None),
            P(),
            P(),
            P(),
            P(),
        ),
        out_specs=(
            P("energy", "dom", None, None, None),
            P("energy", "dom", None),
            P("energy", "dom", None),
        ),
        check_vma=False,
    )
```

profile of v0, /device:TPU:0, one launch (start us, length us, event | category | flops | bytes accessed | tf_op | source)
XLA Modules:
  0.0 668.7 jit_solution(12080986901835495355)
XLA Ops:
  1.3 5.0 collective-permute-start.2
  6.3 2.6 collective-permute-start.3
  8.9 2.1 collective-permute-start.4
  11.0 1.8 collective-permute-start.5
  40.4 1.5 collective-permute-start.9
  42.0 2.6 collective-permute-done.7
  44.6 1.4 collective-permute-done.8
  46.0 3.3 collective-permute-done.9
  49.3 8.1 %add_multiply_fusion = (f32[1,2,128]{2,1,0:T(2,128)S(1)}, f32[1,2,128]{2,1,0:T(2,128)}, f32[1,2,128]{2,1,0:T(2,128)}) fusion(f32[2,9,2,128]{3,2,1,0:T(2,128)S(1)} %constant_dynamic-update-slice_fusion.2, s32[]{:T(128)S(6)} %add.911, s32[]{:T(128)S(6)} %select_n.115, f32[]{:T(128)} %bitcast.113, s32[]{:T(128)S(6)} %select_n.116, f32[]{:T(128)} %bitcast.110, ...), kind=kLoop, calls=%fused_computation.830 | loop fusion | flops 12288 | bytes 27748 | tf_op jit(solution)/shard_map/mul | solution.py:114
  58.8 11.7 %custom-call.45 = f32[1,128,128]{2,1,0:T(8,128)S(1)} custom-call(f32[1,128,128]{2,1,0:T(8,128)S(1)} %cholesky.493), custom_call_target="Cholesky" | custom-call | tf_op jit(solution)/shard_map/jit(cholesky)/cholesky | solution.py:64
  70.6 9.8 %custom-call.46 = f32[1,1,128,128]{2,3,1,0:T(8,128)S(1)} custom-call(f32[1,1,128,128]{3,2,1,0:T(8,128)S(1)} %get-tuple-element.567), custom_call_target="InvertDiagBlocksLowerTriangular" | custom-call | tf_op jit(solution)/shard_map/jit(cholesky)/cholesky | solution.py:64
  80.9 11.7 %custom-call.47 = f32[1,128,128]{2,1,0:T(8,128)S(1)} custom-call(f32[1,128,128]{2,1,0:T(8,128)S(1)} %fusion.170), custom_call_target="Cholesky" | custom-call | tf_op jit(solution)/shard_map/jit(cholesky)/cholesky | solution.py:64
  95.3 3.9 while.38
  99.2 20.1 %custom-call.48 = f32[2,128,128]{1,2,0:T(8,128)S(1)} custom-call(f32[2,128,128]{2,1,0:T(8,128)S(1)} %get-tuple-element.408), custom_call_target="InvertDiagBlocksLowerTriangular" | custom-call | tf_op jit(solution)/shard_map/jit(_cho_solve)/triangular_solve | solution.py:65
  126.0 11.7 %custom-call.49 = f32[1,128,128]{2,1,0:T(8,128)S(1)} custom-call(f32[1,128,128]{2,1,0:T(8,128)S(1)} %cholesky.496), custom_call_target="Cholesky" | custom-call | tf_op jit(solution)/shard_map/jit(cholesky)/cholesky | solution.py:64
  137.8 9.8 %custom-call.50 = f32[1,1,128,128]{2,3,1,0:T(8,128)S(1)} custom-call(f32[1,1,128,128]{3,2,1,0:T(8,128)S(1)} %get-tuple-element.563), custom_call_target="InvertDiagBlocksLowerTriangular" | custom-call | tf_op jit(solution)/shard_map/jit(cholesky)/cholesky | solution.py:64
  148.1 11.9 %custom-call.51 = f32[1,128,128]{2,1,0:T(8,128)S(1)} custom-call(f32[1,128,128]{2,1,0:T(8,128)S(1)} %fusion.171), custom_call_target="Cholesky" | custom-call | tf_op jit(solution)/shard_map/jit(cholesky)/cholesky | solution.py:64
  162.7 4.1 while.39
  163.4 1.3 bitcast_dynamic-update-slice_fusion.27
  165.4 1.3 bitcast_dynamic-update-slice_fusion.27
  166.8 19.7 %custom-call.52 = f32[2,128,128]{1,2,0:T(8,128)S(1)} custom-call(f32[2,128,128]{2,1,0:T(8,128)S(1)} %get-tuple-element.409), custom_call_target="InvertDiagBlocksLowerTriangular" | custom-call | tf_op jit(solution)/shard_map/jit(_cho_solve)/triangular_solve | solution.py:65
  198.7 329.9 %while.37 = (s32[]{:T(128)}, f32[1,2,128,128]{3,2,1,0:T(8,128)S(1)}, f32[1,2,128,128]{3,2,1,0:T(8,128)S(1)}, s32[]{:T(128)}, f32[1,128,128]{2,1,0:T(8,128)S(1)},...) while((s32[]{:T(128)}, ...), condition=%wide.region_9.12_spmd.clone.clone, body=%wide.region_4.11_spmd.clone.sunk.clone | while | flops 2016903680 | bytes 27726664 | solution.py:184
  222.2 68.4 %conditional.8 = (f32[1,2,128,128]{3,2,1,0:T(8,128)S(1)}) conditional(s32[]{:T(128)} %convert_element_type.62, () %tuple.207, (f32[1,2,128,128]{3,2,1,0:T(8,128)S(1)}, f32[1,128,128]{2,1,0:T(8,128)S(1)}, f32[1,128,128]{2,1,0:T(8,128)S(1)}, f32[1,2,128,128]{2,3,1,0:T(8,128)S(1)}, f32[1,128,128]{2,1,0:T(8,128)S(1)}, ...), branch_computations={%region_5.7_spmd, %region_6.8_spmd} | conditional | flops 1008353536 | bytes 12683455 | solution.py:174
  224.0 11.7 %custom-call.37 = f32[1,128,128]{2,1,0:T(8,128)S(1)} custom-call(f32[1,128,128]{2,1,0:T(8,128)S(1)} %cholesky.487), custom_call_target="Cholesky" | custom-call | tf_op jit(solution)/shard_map/while/body/eval_jaxpr/cond/branch_1_fun/jit(cholesky)/cholesky | solution.py:64
  235.8 9.8 %custom-call.38 = f32[1,1,128,128]{2,3,1,0:T(8,128)S(1)} custom-call(f32[1,1,128,128]{3,2,1,0:T(8,128)S(1)} %get-tuple-element.515), custom_call_target="InvertDiagBlocksLowerTriangular" | custom-call | tf_op jit(solution)/shard_map/while/body/eval_jaxpr/cond/branch_1_fun/jit(cholesky)/cholesky | solution.py:64
  246.1 11.7 %custom-call.39 = f32[1,128,128]{2,1,0:T(8,128)S(1)} custom-call(f32[1,128,128]{2,1,0:T(8,128)S(1)} %fusion.6), custom_call_target="Cholesky" | custom-call | tf_op jit(solution)/shard_map/while/body/eval_jaxpr/cond/branch_1_fun/jit(cholesky)/cholesky | solution.py:64
  260.0 4.1 while.35
  260.6 1.3 bitcast_dynamic-update-slice_fusion.24
  264.0 19.7 %custom-call.40 = f32[2,128,128]{1,2,0:T(8,128)S(1)} custom-call(f32[2,128,128]{2,1,0:T(8,128)S(1)} %get-tuple-element.406), custom_call_target="InvertDiagBlocksLowerTriangular" | custom-call | tf_op jit(solution)/shard_map/while/body/eval_jaxpr/cond/branch_1_fun/jit(_cho_solve)/triangular_solve | solution.py:65
  294.4 4.4 collective-permute-done.1
  298.9 69.8 %collective-permute-start = (f32[1,2,128,128]{3,2,1,0:T(8,128)S(1)}, f32[1,2,128,128]{3,2,1,0:T(8,128)S(1)}, u32[]{:S(2)}, u32[]{:S(2)}) collective-permute-start(f32[1,2,128,128]{3,2,1,0:T(8,128)S(1)} %get-tuple-element.1089), channel_id=1, source_target_pairs={{0,1},{1,2},{2,3},{4,5},{5,6},{6,7},{8,9},{9,10},{10,11},{12,13},{... | collective-permute-start | bytes 393224 | tf_op jit(solution)/shard_map/while/body/eval_jaxpr/ppermute | solution.py:18
  371.3 4.4 collective-permute-done.1
  375.8 1.9 collective-permute-start
  380.2 139.6 %collective-permute-done.1 = f32[1,2,128,128]{3,2,1,0:T(8,128)S(1)} collective-permute-done((f32[1,2,128,128]{3,2,1,0:T(8,128)S(1)}, f32[1,2,128,128]{3,2,1,0:T(8,128)S(1)}, u32[]{:S(2)}, u32[]{:S(2)}) %collective-permute-start.1) | collective-permute-done | bytes 131104 | tf_op jit(solution)/shard_map/while/body/eval_jaxpr/ppermute | solution.py:18
  532.2 11.7 %custom-call.53 = f32[1,128,128]{2,1,0:T(8,128)S(1)} custom-call(f32[1,128,128]{2,1,0:T(8,128)S(1)} %cholesky.499), custom_call_target="Cholesky" | custom-call | tf_op jit(solution)/shard_map/jit(cholesky)/cholesky | solution.py:64
  544.0 9.8 %custom-call.54 = f32[1,1,128,128]{2,3,1,0:T(8,128)S(1)} custom-call(f32[1,1,128,128]{3,2,1,0:T(8,128)S(1)} %get-tuple-element.559), custom_call_target="InvertDiagBlocksLowerTriangular" | custom-call | tf_op jit(solution)/shard_map/jit(cholesky)/cholesky | solution.py:64
  554.3 11.7 %custom-call.55 = f32[1,128,128]{2,1,0:T(8,128)S(1)} custom-call(f32[1,128,128]{2,1,0:T(8,128)S(1)} %fusion.172), custom_call_target="Cholesky" | custom-call | tf_op jit(solution)/shard_map/jit(cholesky)/cholesky | solution.py:64
  569.5 4.0 while.40
  570.1 1.4 bitcast_dynamic-update-slice_fusion.28
  572.1 1.4 bitcast_dynamic-update-slice_fusion.28
  573.5 19.7 %custom-call.56 = f32[2,128,128]{1,2,0:T(8,128)S(1)} custom-call(f32[2,128,128]{2,1,0:T(8,128)S(1)} %get-tuple-element.410), custom_call_target="InvertDiagBlocksLowerTriangular" | custom-call | tf_op jit(solution)/shard_map/jit(_cho_solve)/triangular_solve | solution.py:65
  600.1 11.7 %custom-call.57 = f32[1,128,128]{2,1,0:T(8,128)S(1)} custom-call(f32[1,128,128]{2,1,0:T(8,128)S(1)} %cholesky.502), custom_call_target="Cholesky" | custom-call | tf_op jit(solution)/shard_map/jit(cholesky)/cholesky | solution.py:64
  611.9 9.8 %custom-call.58 = f32[1,1,128,128]{2,3,1,0:T(8,128)S(1)} custom-call(f32[1,1,128,128]{3,2,1,0:T(8,128)S(1)} %get-tuple-element.555), custom_call_target="InvertDiagBlocksLowerTriangular" | custom-call | tf_op jit(solution)/shard_map/jit(cholesky)/cholesky | solution.py:64
  622.2 12.0 %custom-call.59 = f32[1,128,128]{2,1,0:T(8,128)S(1)} custom-call(f32[1,128,128]{2,1,0:T(8,128)S(1)} %fusion.173), custom_call_target="Cholesky" | custom-call | tf_op jit(solution)/shard_map/jit(cholesky)/cholesky | solution.py:64
  636.8 4.0 while.41
  637.4 1.4 bitcast_dynamic-update-slice_fusion.29
  639.4 1.4 bitcast_dynamic-update-slice_fusion.29
  640.8 19.7 %custom-call.60 = f32[2,128,128]{1,2,0:T(8,128)S(1)} custom-call(f32[2,128,128]{2,1,0:T(8,128)S(1)} %get-tuple-element.411), custom_call_target="InvertDiagBlocksLowerTriangular" | custom-call | tf_op jit(solution)/shard_map/jit(_cho_solve)/triangular_solve | solution.py:65
  (385 shorter events, 87.5 us)
Async XLA Ops:
  0.6 0.7 copy-start.9
  0.6 0.7 copy-start.8
  1.3 11.5 %copy-start.5 = (s32[6]{0:T(128)S(1)}, s32[6]{0:T(128)}, u32[]{:S(2)}) copy-start(s32[6]{0:T(128)} %param.22) | copy-start | bytes 76
  1.3 36.4 %collective-permute-start.2 = (f32[2,1,2,128]{3,2,1,0:T(2,128)S(1)}, f32[2,1,2,128]{3,2,1,0:T(2,128)S(1)}, u32[]{:S(2)}, u32[]{:S(2)}) collective-permute-start(f32[2,1,2,128]{3,2,1,0:T(2,128)S(1)} %pad_maximum_fusion.3), channel_id=1, source_target_pairs={{0,16},{4,20},{8,24},{12,28},{1,17},{5,21},{9,25},{13,29},{2,18},{... | collective-permute-start | bytes 6152 | tf_op jit(solution)/shard_map/ppermute | solution.py:18
  6.3 32.7 %collective-permute-start.3 = (f32[2,1,2,128]{3,2,1,0:T(2,128)S(1)}, f32[2,1,2,128]{3,2,1,0:T(2,128)S(1)}, u32[]{:S(2)}, u32[]{:S(2)}) collective-permute-start(f32[2,1,2,128]{3,2,1,0:T(2,128)S(1)} %pad_maximum_fusion.3), channel_id=1, source_target_pairs={{0,12},{4,16},{8,20},{12,24},{16,28},{1,13},{5,17},{9,21},{13,25},... | collective-permute-start | bytes 6152 | tf_op jit(solution)/shard_map/ppermute | solution.py:18
  8.9 31.5 %collective-permute-start.4 = (f32[2,1,2,128]{3,2,1,0:T(2,128)S(1)}, f32[2,1,2,128]{3,2,1,0:T(2,128)S(1)}, u32[]{:S(2)}, u32[]{:S(2)}) collective-permute-start(f32[2,1,2,128]{3,2,1,0:T(2,128)S(1)} %pad_maximum_fusion.3), channel_id=1, source_target_pairs={{0,8},{4,12},{8,16},{12,20},{16,24},{20,28},{1,9},{5,13},{9,17},{1... | collective-permute-start | bytes 6152 | tf_op jit(solution)/shard_map/ppermute | solution.py:18
  11.0 30.9 %collective-permute-start.5 = (f32[2,1,2,128]{3,2,1,0:T(2,128)S(1)}, f32[2,1,2,128]{3,2,1,0:T(2,128)S(1)}, u32[]{:S(2)}, u32[]{:S(2)}) collective-permute-start(f32[2,1,2,128]{3,2,1,0:T(2,128)S(1)} %pad_maximum_fusion.3), channel_id=1, source_target_pairs={{0,4},{4,8},{8,12},{12,16},{16,20},{20,24},{24,28},{1,5},{5,9},{9,... | collective-permute-start | bytes 6152 | tf_op jit(solution)/shard_map/ppermute | solution.py:18
  30.0 1.3 copy-start.1
  30.0 3.9 copy-start.4
  31.9 0.7 copy-start.6
  31.9 1.3 copy-start.7
  33.9 1.0 copy-start
  36.4 5.5 collective-permute-start.6
  37.7 6.8 %collective-permute-start.7 = (f32[2,1,2,128]{3,2,1,0:T(2,128)S(1)}, f32[2,1,2,128]{3,2,1,0:T(2,128)S(1)}, u32[]{:S(2)}, u32[]{:S(2)}) collective-permute-start(f32[2,1,2,128]{3,2,1,0:T(2,128)S(1)} %pad_maximum_fusion.3), channel_id=1, source_target_pairs={{8,0},{12,4},{16,8},{20,12},{24,16},{28,20},{9,1},{13,5},{17,9},{2... | collective-permute-start | bytes 6152 | tf_op jit(solution)/shard_map/ppermute | solution.py:18
  39.1 6.9 %collective-permute-start.8 = (f32[2,1,2,128]{3,2,1,0:T(2,128)S(1)}, f32[2,1,2,128]{3,2,1,0:T(2,128)S(1)}, u32[]{:S(2)}, u32[]{:S(2)}) collective-permute-start(f32[2,1,2,128]{3,2,1,0:T(2,128)S(1)} %pad_maximum_fusion.3), channel_id=1, source_target_pairs={{12,0},{16,4},{20,8},{24,12},{28,16},{13,1},{17,5},{21,9},{25,13},... | collective-permute-start | bytes 6152 | tf_op jit(solution)/shard_map/ppermute | solution.py:18
  40.4 8.9 %collective-permute-start.9 = (f32[2,1,2,128]{3,2,1,0:T(2,128)S(1)}, f32[2,1,2,128]{3,2,1,0:T(2,128)S(1)}, u32[]{:S(2)}, u32[]{:S(2)}) collective-permute-start(f32[2,1,2,128]{3,2,1,0:T(2,128)S(1)} %pad_maximum_fusion.3), channel_id=1, source_target_pairs={{16,0},{20,4},{24,8},{28,12},{17,1},{21,5},{25,9},{29,13},{18,2},{... | collective-permute-start | bytes 6152 | tf_op jit(solution)/shard_map/ppermute | solution.py:18
  57.5 0.6 copy-start.2
  166.7 19.7 %copy-start.10 = (s32[2,2]{1,0:T(2,128)}, s32[2,2]{1,0:T(2,128)S(1)}, u32[]{:S(2)}) copy-start(s32[2,2]{1,0:T(2,128)S(1)} %get-tuple-element.1118) | copy-start | bytes 52
  290.5 3.8 collective-permute-start
  291.9 6.9 %collective-permute-start.1 = (f32[1,2,128,128]{3,2,1,0:T(8,128)S(1)}, f32[1,2,128,128]{3,2,1,0:T(8,128)S(1)}, u32[]{:S(2)}, u32[]{:S(2)}) collective-permute-start(f32[1,2,128,128]{3,2,1,0:T(8,128)S(1)} %get-tuple-element.1090), channel_id=1, source_target_pairs={{1,0},{2,1},{3,2},{5,4},{6,5},{7,6},{9,8},{10,9},{11,10},{13,12},{... | collective-permute-start | bytes 393224 | tf_op jit(solution)/shard_map/while/body/eval_jaxpr/ppermute | solution.py:18
  298.9 72.3 %collective-permute-start = (f32[1,2,128,128]{3,2,1,0:T(8,128)S(1)}, f32[1,2,128,128]{3,2,1,0:T(8,128)S(1)}, u32[]{:S(2)}, u32[]{:S(2)}) collective-permute-start(f32[1,2,128,128]{3,2,1,0:T(8,128)S(1)} %get-tuple-element.1089), channel_id=1, source_target_pairs={{0,1},{1,2},{2,3},{4,5},{5,6},{6,7},{8,9},{9,10},{10,11},{12,13},{... | collective-permute-start | bytes 393224 | tf_op jit(solution)/shard_map/while/body/eval_jaxpr/ppermute | solution.py:18
  368.8 6.9 %collective-permute-start.1 = (f32[1,2,128,128]{3,2,1,0:T(8,128)S(1)}, f32[1,2,128,128]{3,2,1,0:T(8,128)S(1)}, u32[]{:S(2)}, u32[]{:S(2)}) collective-permute-start(f32[1,2,128,128]{3,2,1,0:T(8,128)S(1)} %get-tuple-element.1090), channel_id=1, source_target_pairs={{1,0},{2,1},{3,2},{5,4},{6,5},{7,6},{9,8},{10,9},{11,10},{13,12},{... | collective-permute-start | bytes 393224 | tf_op jit(solution)/shard_map/while/body/eval_jaxpr/ppermute | solution.py:18
  375.8 4.4 collective-permute-start
  377.8 142.1 %collective-permute-start.1 = (f32[1,2,128,128]{3,2,1,0:T(8,128)S(1)}, f32[1,2,128,128]{3,2,1,0:T(8,128)S(1)}, u32[]{:S(2)}, u32[]{:S(2)}) collective-permute-start(f32[1,2,128,128]{3,2,1,0:T(8,128)S(1)} %get-tuple-element.1090), channel_id=1, source_target_pairs={{1,0},{2,1},{3,2},{5,4},{6,5},{7,6},{9,8},{10,9},{11,10},{13,12},{... | collective-permute-start | bytes 393224 | tf_op jit(solution)/shard_map/while/body/eval_jaxpr/ppermute | solution.py:18
  530.7 0.8 copy-start.3
  568.8 0.7 copy-start.11
where the time goes:
time: 672 us; the launch traced here: 669 us
  other arithmetic  282 us (42%)
  waiting for transfers between devices  159 us (24%)
  starting transfers between devices  93.8 us (14%)
  matrix products  48.5 us (7%)
  loops' own time  34.4 us (5%)
  local copies, waits for them, and re-layouts  27.4 us (4%)
  between operations  23.4 us (3%)
    another operation x36, other arithmetic, invert(): factor = jnp.linalg.cholesky(normal_matrix)  173 us
    ppermute x14, waiting for transfers between devices, passed_along(): return lax.ppermute(value, axis, pairs)  159 us
    another operation x13, other arithmetic, invert(): jax.scipy.linalg.cho_solve((factor, True), transposed[..., :order_size])  99 us
    ppermute x14, starting transfers between devices, passed_along(): return lax.ppermute(value, axis, pairs)  93.8 us
    another operation x1, loops' own time, local(): lax.fori_loop(0, partitions - 1, relay_turn, (zero_block, zero_block))  32.4 us
    another operation x36, local copies, waits for them, and re-layouts, invert(): jax.scipy.linalg.cho_solve((factor, True), transposed[..., :order_size])  19.9 us
  transfers between devices with their start and end apart: 14, of which 9 were waited for; matrix products, arithmetic and copies ran while one was open for 1% of the time, Pallas kernels for 0%

commit v1 on v0

v1 whole, which is shorter than its diff:
```python
import functools

import jax
import jax.numpy as jnp
from jax import lax
from jax.experimental import pallas as pl
from jax.experimental.pallas import tpu as pltpu
from jax.sharding import PartitionSpec as P

MODES = 6
SMAX = 4
N = 128
H = 64
B = 8

energy_low = -1.0
energy_span = 2.0
damping = 0.02

MESH = pl.DeviceIdType.MESH


def product(a, b):
    h = b.shape[1] // 2
    turned_rows = jnp.concatenate([-b[:, h:], b[:, :h]], axis=1)
    return jnp.dot(
        a,
        jnp.concatenate([b, turned_rows], axis=0),
        precision=lax.Precision.HIGHEST,
        preferred_element_type=jnp.float32,
    )


def adjoint(a):
    return jnp.concatenate([a[:, :N].T, -a[:, N:].T], axis=1)


def identity():
    row = lax.broadcasted_iota(jnp.int32, (N, 2 * N), 0)
    lane = lax.broadcasted_iota(jnp.int32, (N, 2 * N), 1)
    return jnp.where(row == lane, 1.0, 0.0)


def times_i(a):
    r = pltpu.roll(a, H, axis=1)
    return jnp.where(lax.broadcasted_iota(jnp.int32, a.shape, 1) < H, -r, r)


def invert_half(x):
    shape = (B, N)
    row = lax.broadcasted_iota(jnp.int32, shape, 0)
    lane = lax.broadcasted_iota(jnp.int32, shape, 1)
    column = lane % H
    groups = [x[i * B : (i + 1) * B] for i in range(H // B)]
    count = len(groups)

    def along_lanes(v, c):
        return jnp.broadcast_to(v[:, c : c + 1], shape)

    def along_rows(v, k):
        return jnp.broadcast_to(v[k : k + 1], shape)

    for p in range(count):
        panel = groups[p]
        turned = times_i(panel)
        br = [along_lanes(panel, p * B + j) for j in range(B)]
        bi = [along_lanes(panel, H + p * B + j) for j in range(B)]
        for k in range(B):
            own = row == k
            qr = along_rows(br[k], k)
            qi = along_rows(bi[k], k)
            s = 1.0 / (qr * qr + qi * qi)
            vr = qr * s
            vi = -qi * s
            mr = jnp.where(own, 0.0, br[k])
            mi = jnp.where(own, 0.0, bi[k])
            here = column == p * B + k
            panel = jnp.where(here, jnp.where(own & (lane < H), 1.0, 0.0), panel)
            turned = jnp.where(here, jnp.where(own & (lane >= H), 1.0, 0.0), turned)
            y = along_rows(panel, k)
            ty = along_rows(turned, k)
            r = y * vr + ty * vi
            tr = ty * vr - y * vi
            panel = jnp.where(own, r, panel - (mr * r + mi * tr))
            turned = jnp.where(own, tr, turned - (mr * tr - mi * r))
            for j in range(k + 1, B):
                yr = along_rows(br[j], k)
                yi = along_rows(bi[j], k)
                rr = yr * vr - yi * vi
                ri = yr * vi + yi * vr
                br[j] = jnp.where(own, rr, br[j] - (mr * rr - mi * ri))
                bi[j] = jnp.where(own, ri, bi[j] - (mr * ri + mi * rr))
        groups[p] = panel
        inside = (column >= p * B) & (column < (p + 1) * B)
        rr = [along_rows(panel, j) for j in range(B)]
        ri = [along_rows(turned, j) for j in range(B)]
        for t in range(1, count):
            g = (p + t) % count
            old = groups[g]
            new = jnp.where(inside, 0.0, old)
            for j in range(B):
                new = new - (
                    along_lanes(old, p * B + j) * rr[j] + along_lanes(old, H + p * B + j) * ri[j]
                )
            groups[g] = new
    return jnp.concatenate(groups, axis=0)


def quarter(x, i, j):
    rows = x[i * H : (i + 1) * H]
    return jnp.concatenate(
        [rows[:, j * H : (j + 1) * H], rows[:, N + j * H : N + (j + 1) * H]], axis=1
    )


def invert_into(x, out_ref):
    a, b, c, d = quarter(x, 0, 0), quarter(x, 0, 1), quarter(x, 1, 0), quarter(x, 1, 1)
    e = invert_half(a)
    f = product(e, b)
    g = product(c, e)
    s = invert_half(d - product(c, f))
    fs = product(f, s)
    first = e + product(fs, g)
    across = -fs
    back = -product(s, g)
    out_ref[:H] = jnp.concatenate(
        [first[:, :H], across[:, :H], first[:, H:], across[:, H:]], axis=1
    )
    out_ref[H:] = jnp.concatenate([back[:, :H], s[:, :H], back[:, H:], s[:, H:]], axis=1)


def kernel(
    energy_count,
    partitions,
    steps_ref,
    emission_ref,
    absorption_ref,
    lesser_ref,
    greater_ref,
    ham_ref,
    coupling_ref,
    lead_ref,
    green_ref,
    in_ref,
    out_ref,
    own_ref,
    window_ref,
    received,
    outgoing,
    a_first,
    a_second,
    c_fs,
    c_sf,
    w,
    wd,
    f_ref,
    u_ref,
    t_ref,
    s_ref,
    g_ref,
    th_ref,
    ht_ref,
    hb_ref,
    sig_ref,
    y_ref,
    uy_ref,
    q_ref,
    x_ref,
    r_ref,
    occ_send,
    occ_recv,
    dom_send,
    dom_recv,
):
    energy = lax.axis_index("energy")
    dom = lax.axis_index("dom")
    half = (2 * dom >= partitions).astype(jnp.int32)
    left_half = half == 0
    right_half = half == 1
    has_early = jnp.where(left_half, dom, partitions - 1 - dom) > 0
    offsets = [o for o in range(-SMAX, SMAX + 1) if o != 0]

    def in_range(o):
        return (energy + o >= 0) & (energy + o < energy_count)

    barrier = pltpu.get_barrier_semaphore()
    greeted = jnp.int32(0)
    for o in offsets:
        there = in_range(o)
        greeted = greeted + there.astype(jnp.int32)

        @pl.when(there)
        def _():
            pl.semaphore_signal(
                barrier, inc=1, device_id={"energy": energy + o}, device_id_type=MESH
            )

    for o in (-1, 1):
        there = (dom + o >= 0) & (dom + o < partitions)
        greeted = greeted + there.astype(jnp.int32)

        @pl.when(there)
        def _():
            pl.semaphore_signal(barrier, inc=1, device_id={"dom": dom + o}, device_id_type=MESH)

    own_ref[0:2] = lesser_ref[0]
    own_ref[2:4] = greater_ref[0]
    own_ref[4:8] = jnp.zeros((4, N), jnp.float32)
    pl.semaphore_wait(barrier, greeted)

    def occupancy_copy(number, o):
        return pltpu.make_async_remote_copy(
            src_ref=own_ref,
            dst_ref=window_ref.at[len(offsets) - 1 - number],
            send_sem=occ_send.at[number],
            recv_sem=occ_recv.at[len(offsets) - 1 - number],
            device_id={"energy": energy + o},
            device_id_type=MESH,
        )

    for number, o in enumerate(offsets):
        there = in_range(o)

        @pl.when(there)
        def _():
            occupancy_copy(number, o).start()

        @pl.when(jnp.logical_not(there))
        def _():
            window_ref[number] = jnp.zeros((8, N), jnp.float32)

    link = jnp.concatenate([coupling_ref[1, 0], coupling_ref[1, 1]], axis=1)
    link_adjoint = adjoint(link)
    outer = jnp.concatenate([coupling_ref[0, 0], coupling_ref[0, 1]], axis=1)
    outer_adjoint = adjoint(outer)
    w[...] = outer
    wd[...] = outer_adjoint

    @pl.when(left_half)
    def _():
        c_fs[...] = link
        c_sf[...] = link_adjoint

    @pl.when(right_half)
    def _():
        c_fs[...] = link_adjoint
        c_sf[...] = link

    @pl.when(has_early)
    def _():
        x_ref[...] = jnp.zeros((N, 2 * N), jnp.float32)

    def half_i(a):
        return jnp.concatenate([-0.5 * a[:, N:], 0.5 * a[:, :N]], axis=1)

    @pl.when(dom == 0)
    def _():
        x_ref[...] = half_i(product(wd[...], w[...]))

    @pl.when(dom == partitions - 1)
    def _():
        lead = jnp.concatenate([lead_ref[0], lead_ref[1]], axis=1)
        x_ref[...] = half_i(product(lead, adjoint(lead)))

    for number, o in enumerate(offsets):

        @pl.when(in_range(o))
        def _():
            occupancy_copy(len(offsets) - 1 - number, -o).wait_recv()

    scattering_in = jnp.zeros((2, N), jnp.float32)
    scattering_out = jnp.zeros((2, N), jnp.float32)
    for step in range(1, SMAX + 1):
        emission = jnp.float32(0.0)
        absorption = jnp.float32(0.0)
        for m in range(MODES):
            chosen = steps_ref[m] == step
            emission = emission + jnp.where(chosen, emission_ref[m], 0.0)
            absorption = absorption + jnp.where(chosen, absorption_ref[m], 0.0)
        above = window_ref[offsets.index(step)]
        below = window_ref[offsets.index(-step)]
        scattering_in = scattering_in + emission * above[0:2] + absorption * below[0:2]
        scattering_out = scattering_out + emission * below[2:4] + absorption * above[2:4]
    in_ref[0] = scattering_in
    out_ref[0] = scattering_out
    broadening = 0.5 * (scattering_in + scattering_out)

    position = jnp.full((N, N), energy, jnp.int32).astype(jnp.float32)
    energy_value = energy_low + energy_span * (position + 0.5) / energy_count
    unit = identity()[:, :N]

    def system(b):
        real_part = unit * energy_value - ham_ref[b, 0]
        imag_part = unit * (damping + broadening[b : b + 1]) - ham_ref[b, 1]
        return jnp.concatenate([real_part, imag_part], axis=1)

    block_0 = system(0)
    block_1 = system(1)

    @pl.when(left_half)
    def _():
        a_first[...] = block_0 + x_ref[...]
        a_second[...] = block_1

    @pl.when(right_half)
    def _():
        a_first[...] = block_1 + x_ref[...]
        a_second[...] = block_0

    def early_copy():
        return pltpu.make_async_remote_copy(
            src_ref=outgoing.at[0],
            dst_ref=received.at[half],
            send_sem=dom_send.at[0],
            recv_sem=dom_recv.at[half],
            device_id={"dom": dom + 1 - 2 * half},
            device_id_type=MESH,
        )

    def late_copy():
        return pltpu.make_async_remote_copy(
            src_ref=outgoing.at[1],
            dst_ref=received.at[1 - half],
            send_sem=dom_send.at[1],
            recv_sem=dom_recv.at[1 - half],
            device_id={"dom": dom - 1 + 2 * half},
            device_id_type=MESH,
        )

    def wrap_out(v):
        return product(product(w[...], v), wd[...])

    def wrap_in(v):
        return product(product(wd[...], v), w[...])

    def send_early(v):
        @pl.when(left_half)
        def _():
            outgoing[0] = v

        @pl.when(right_half)
        def _():
            outgoing[0] = wrap_out(v)

        early_copy().start()

    def stage(number, carry):
        @pl.when(has_early | ((number != 2) & (number != 4)))
        def _():
            @pl.when(number == 0)
            def _():
                x_ref[...] = a_first[...]

            @pl.when(number == 1)
            def _():
                x_ref[...] = s_ref[...]

            @pl.when(number == 2)
            def _():
                early_copy().wait_recv()

                @pl.when(left_half)
                def _():
                    sig_ref[...] = wrap_in(received[0])

                @pl.when(right_half)
                def _():
                    sig_ref[...] = received[1]

                x_ref[...] = identity() - product(hb_ref[...], sig_ref[...])

            @pl.when(number == 3)
            def _():
                late_copy().wait_recv()

                @pl.when(left_half)
                def _():
                    x_ref[...] = s_ref[...] - received[1]

                @pl.when(right_half)
                def _():
                    x_ref[...] = s_ref[...] - wrap_in(received[0])

            @pl.when(number == 4)
            def _():
                x_ref[...] = identity() - product(q_ref[...], sig_ref[...])

            invert_into(x_ref[...], r_ref)

            @pl.when(number == 0)
            def _():
                f = r_ref[...]
                t = product(c_sf[...], f)
                f_ref[...] = f
                t_ref[...] = t
                s_ref[...] = a_second[...] - product(t, c_fs[...])
                u_ref[...] = product(f, c_fs[...])

            @pl.when(number == 1)
            def _():
                g = r_ref[...]
                g_ref[...] = g

                @pl.when(jnp.logical_not(has_early))
                def _():
                    send_early(g)

                @pl.when(has_early)
                def _():
                    ht = product(u_ref[...], g)
                    ht_ref[...] = ht
                    hb_ref[...] = f_ref[...] + product(ht, t_ref[...])
                    th_ref[...] = product(g, t_ref[...])

            @pl.when(number == 2)
            def _():
                z = product(sig_ref[...], r_ref[...])
                send_early(g_ref[...] + product(product(th_ref[...], z), ht_ref[...]))

            @pl.when(number == 3)
            def _():
                y = r_ref[...]
                uy = product(u_ref[...], y)
                q = f_ref[...] + product(uy, t_ref[...])
                y_ref[...] = y
                uy_ref[...] = uy
                q_ref[...] = q

                @pl.when(has_early)
                def _():
                    @pl.when(left_half)
                    def _():
                        outgoing[1] = wrap_out(q)

                    @pl.when(right_half)
                    def _():
                        outgoing[1] = q

                    late_copy().start()

            @pl.when(number == 4)
            def _():
                m = r_ref[...]
                y = y_ref[...]
                z = product(sig_ref[...], m)
                yt = product(y, t_ref[...])
                y_ref[...] = y + product(product(yt, z), uy_ref[...])
                q_ref[...] = product(m, q_ref[...])

        return carry

    lax.fori_loop(0, 5, stage, 0)

    def put(block, v):
        green_ref[0, block, 0] = v[:, :N]
        green_ref[0, block, 1] = v[:, N:]

    @pl.when(left_half)
    def _():
        put(0, q_ref[...])
        put(1, y_ref[...])

    @pl.when(right_half)
    def _():
        put(0, y_ref[...])
        put(1, q_ref[...])

    for number, o in enumerate(offsets):

        @pl.when(in_range(o))
        def _():
            occupancy_copy(number, o).wait_send()

    early_copy().wait_send()

    @pl.when(has_early)
    def _():
        late_copy().wait_send()


def local(
    lesser_occupancy,
    greater_occupancy,
    hamiltonian,
    couplings,
    right_lead,
    phonon_steps,
    emission_strength,
    absorption_strength,
):
    whole = pl.BlockSpec(memory_space=pltpu.VMEM)
    scalars = pl.BlockSpec(memory_space=pltpu.SMEM)
    matrix = pltpu.VMEM((N, 2 * N), jnp.float32)
    pair = pltpu.VMEM((2, N, 2 * N), jnp.float32)
    reach = 2 * SMAX
    return pl.pallas_call(
        functools.partial(kernel, lax.axis_size("energy"), lax.axis_size("dom")),
        out_shape=(
            jax.ShapeDtypeStruct((1, 2, 2, N, N), jnp.float32),
            jax.ShapeDtypeStruct((1, 2, N), jnp.float32),
            jax.ShapeDtypeStruct((1, 2, N), jnp.float32),
        ),
        in_specs=[scalars] * 3 + [whole] * 5,
        out_specs=(whole,) * 3,
        scratch_shapes=[
            pltpu.VMEM((8, N), jnp.float32),
            pltpu.VMEM((reach, 8, N), jnp.float32),
            pair,
            pair,
        ]
        + [matrix] * 20
        + [
            pltpu.SemaphoreType.DMA((reach,)),
            pltpu.SemaphoreType.DMA((reach,)),
            pltpu.SemaphoreType.DMA((2,)),
            pltpu.SemaphoreType.DMA((2,)),
        ],
        compiler_params=pltpu.CompilerParams(
            collective_id=0, has_side_effects=True, vmem_limit_bytes=40 * 2**20
        ),
    )(
        phonon_steps,
        emission_strength,
        absorption_strength,
        lesser_occupancy,
        greater_occupancy,
        hamiltonian,
        couplings,
        right_lead,
    )


def solution(mesh):
    return jax.shard_map(
        local,
        mesh=mesh,
        in_specs=(
            P("energy", "dom", None),
            P("energy", "dom", None),
            P("dom", None, None, None),
            P("dom", None, None, None),
            P(),
            P(),
            P(),
            P(),
        ),
        out_specs=(
            P("energy", "dom", None, None, None),
            P("energy", "dom", None),
            P("energy", "dom", None),
        ),
        check_vma=False,
    )
```

time: 672 us -> 65.3 us (0.10)
  other arithmetic: 282 us -> 0 us
  waiting for transfers between devices: 159 us -> 0 us
  starting transfers between devices: 93.8 us -> 0 us
  Pallas kernels: 0 us -> 56.4 us
  matrix products: 48.5 us -> 0 us
  loops' own time: 34.4 us -> 0 us
  between operations: 23.4 us -> 0.66 us
  local copies, waits for them, and re-layouts: 27.4 us -> 7.95 us
    another operation x54 -> x0, other arithmetic: 273 us -> none  [the longest x36 173 us: invert(): factor = jnp.linalg.cholesky(normal_matrix)]
    ppermute x14 -> x0, waiting for transfers between devices: 159 us -> none  [passed_along(): return lax.ppermute(value, axis, pairs)]
    ppermute x14 -> x0, starting transfers between devices: 93.8 us -> none  [passed_along(): return lax.ppermute(value, axis, pairs)]
    pallas_call x0 -> x1, Pallas kernels: none -> 56.4 us  [local(): pl.pallas_call(functools.partial(kernel, lax.axis_size('energy'), lax.axi...]
    dot_general x141 -> x0, matrix products: 38.8 us -> none  [the longest x34 9.63 us: complex_product(): jnp.matmul(left_real, right_imag, precision=highest)]
    another operation x12 -> x0, loops' own time: 34.4 us -> none  [the longest x1 32.4 us: local(): lax.fori_loop(0, partitions - 1, relay_turn, (zero_block, zero_block))]
    another operation x51 -> x0, local copies, waits for them, and re-layouts: 20.1 us -> none  [the longest x36 19.9 us: invert(): jax.scipy.linalg.cho_solve((factor, True), transposed[..., :order_size])]
    another operation x40 -> x0, matrix products: 9.67 us -> none  [the longest x30 7.31 us: invert(): jax.scipy.linalg.cho_solve((factor, True), transposed[..., :order_size])]
  transfers between devices with their start and end apart: 14 -> 0, of which waited for: 9 -> 0; matrix products, arithmetic and copies ran while one was open for 1% -> 0% of each run, Pallas kernels for 0% -> 0%
where the time goes in v1:
time: 65.3 us; the launch traced here: 65 us
  Pallas kernels  56.4 us (86%)
  local copies, waits for them, and re-layouts  7.95 us (12%)
  between operations  0.66 us (1%)
    pallas_call x1, Pallas kernels, local(): pl.pallas_call(functools.partial(kernel, lax.axis_size('energy'), lax.axi...  56.4 us
    unnamed x19, local copies, waits for them, and re-layouts  7.95 us

profile of v1, /device:TPU:0, one launch (start us, length us, event | category | flops | bytes accessed | tf_op | source)
XLA Modules:
  0.0 65.0 jit_solution(15409379263846366464)
XLA Ops:
  0.6 0.0 copy-start
  0.6 0.9 %copy-done = f32[2,2,128,128]{3,2,1,0:T(8,128)S(1)} copy-done((f32[2,2,128,128]{3,2,1,0:T(8,128)S(1)}, f32[2,2,128,128]{3,2,1,0:T(8,128)}, u32[]{:S(2)}) %copy-start) | copy-done | bytes 262168
  1.6 0.0 copy-start.1
  1.6 0.9 %copy-done.1 = f32[2,2,128,128]{3,2,1,0:T(8,128)S(1)} copy-done((f32[2,2,128,128]{3,2,1,0:T(8,128)S(1)}, f32[2,2,128,128]{3,2,1,0:T(8,128)}, u32[]{:S(2)}) %copy-start.1) | copy-done | bytes 262168
  2.5 0.0 copy-start.2
  2.5 0.9 %copy-done.2 = f32[2,128,128]{2,1,0:T(8,128)S(1)} copy-done((f32[2,128,128]{2,1,0:T(8,128)S(1)}, f32[2,128,128]{2,1,0:T(8,128)}, u32[]{:S(2)}) %copy-start.2) | copy-done | bytes 131096
  3.4 0.0 copy-start.3
  3.4 0.7 %copy-done.3 = f32[1,2,128]{2,1,0:T(2,128)S(1)} copy-done((f32[1,2,128]{2,1,0:T(2,128)S(1)}, f32[1,2,128]{2,1,0:T(2,128)}, u32[]{:S(2)}) %copy-start.3) | copy-done | bytes 1048
  4.1 0.0 copy-start.4
  4.1 0.7 %copy-done.4 = f32[1,2,128]{2,1,0:T(2,128)S(1)} copy-done((f32[1,2,128]{2,1,0:T(2,128)S(1)}, f32[1,2,128]{2,1,0:T(2,128)}, u32[]{:S(2)}) %copy-start.4) | copy-done | bytes 1048
  4.8 0.0 copy-start.5
  4.8 0.7 %copy-done.5 = s32[6]{0:T(128)S(1)} copy-done((s32[6]{0:T(128)S(1)}, s32[6]{0:T(128)}, u32[]{:S(2)}) %copy-start.5) | copy-done | bytes 48
  5.5 0.0 copy-start.6
  5.5 0.7 %copy-done.6 = f32[6]{0:T(128)S(1)} copy-done((f32[6]{0:T(128)S(1)}, f32[6]{0:T(128)}, u32[]{:S(2)}) %copy-start.6) | copy-done | bytes 48
  6.1 0.0 copy-start.7
  6.1 0.7 %copy-done.7 = f32[6]{0:T(128)S(1)} copy-done((f32[6]{0:T(128)S(1)}, f32[6]{0:T(128)}, u32[]{:S(2)}) %copy-start.7) | copy-done | bytes 48
  6.8 56.4 %shard_map.103 = (f32[1,2,2,128,128]{4,3,2,1,0:T(8,128)S(1)}, f32[1,2,128]{2,1,0:T(2,128)S(1)}, f32[1,2,128]{2,1,0:T(2,128)S(1)}) custom-call(s32[6]{0:T(128)S(1)} %copy-done.5, f32[6]{0:T(128)S(1)} %copy-done.6, f32[6]{0:T(128)S(1)} %copy-done.7, f32[1,2,128]{2,1,0:T(2,128)S(1)} %copy-done.3, f32[1,2,128]{2,1,0:T(2,128)S(1)} %copy-done.4, ...), custom_call_target="tpu_custom_call" | custom-call | tf_op jit(solution)/shard_map/pallas_call | solution.py:496
  63.2 0.7 %copy.14 = f32[1,2,2,128,128]{4,3,2,1,0:T(8,128)} copy(f32[1,2,2,128,128]{4,3,2,1,0:T(8,128)S(1)} %get-tuple-element.6) | data formatting | bytes 524288
  63.9 0.6 copy.15
  64.4 0.6 copy.16
Async XLA Ops:
  0.6 1.0 %copy-start = (f32[2,2,128,128]{3,2,1,0:T(8,128)S(1)}, f32[2,2,128,128]{3,2,1,0:T(8,128)}, u32[]{:S(2)}) copy-start(f32[2,2,128,128]{3,2,1,0:T(8,128)} %ham_ref.1) | copy-start | bytes 786436
  1.6 0.9 %copy-start.1 = (f32[2,2,128,128]{3,2,1,0:T(8,128)S(1)}, f32[2,2,128,128]{3,2,1,0:T(8,128)}, u32[]{:S(2)}) copy-start(f32[2,2,128,128]{3,2,1,0:T(8,128)} %coupling_ref.1) | copy-start | bytes 786436
  2.5 0.9 %copy-start.2 = (f32[2,128,128]{2,1,0:T(8,128)S(1)}, f32[2,128,128]{2,1,0:T(8,128)}, u32[]{:S(2)}) copy-start(f32[2,128,128]{2,1,0:T(8,128)} %lead_ref.1) | copy-start | bytes 393220
  3.4 0.7 %copy-start.3 = (f32[1,2,128]{2,1,0:T(2,128)S(1)}, f32[1,2,128]{2,1,0:T(2,128)}, u32[]{:S(2)}) copy-start(f32[1,2,128]{2,1,0:T(2,128)} %lesser_ref.1) | copy-start | bytes 3076
  4.1 0.7 %copy-start.4 = (f32[1,2,128]{2,1,0:T(2,128)S(1)}, f32[1,2,128]{2,1,0:T(2,128)}, u32[]{:S(2)}) copy-start(f32[1,2,128]{2,1,0:T(2,128)} %greater_ref.1) | copy-start | bytes 3076
  4.8 0.7 %copy-start.5 = (s32[6]{0:T(128)S(1)}, s32[6]{0:T(128)}, u32[]{:S(2)}) copy-start(s32[6]{0:T(128)} %steps_ref.1) | copy-start | bytes 76
  5.5 0.7 %copy-start.6 = (f32[6]{0:T(128)S(1)}, f32[6]{0:T(128)}, u32[]{:S(2)}) copy-start(f32[6]{0:T(128)} %emission_ref.1) | copy-start | bytes 76
  6.1 0.7 %copy-start.7 = (f32[6]{0:T(128)S(1)}, f32[6]{0:T(128)}, u32[]{:S(2)}) copy-start(f32[6]{0:T(128)} %absorption_ref.1) | copy-start | bytes 76

commit v2 on v1

--- a/solution.py
+++ b/solution.py
@@ -20,15 +20,22 @@
 MESH = pl.DeviceIdType.MESH
 
 
+def parts(v):
+    high = v.astype(jnp.bfloat16)
+    return high, (v - high.astype(jnp.float32)).astype(jnp.bfloat16)
+
+
+def real_product(a, b):
+    a_high, a_low = parts(a)
+    b_high, b_low = parts(b)
+    dot = functools.partial(jnp.dot, preferred_element_type=jnp.float32)
+    return dot(a_high, b_high) + (dot(a_high, b_low) + dot(a_low, b_high))
+
+
 def product(a, b):
     h = b.shape[1] // 2
     turned_rows = jnp.concatenate([-b[:, h:], b[:, :h]], axis=1)
-    return jnp.dot(
-        a,
-        jnp.concatenate([b, turned_rows], axis=0),
-        precision=lax.Precision.HIGHEST,
-        preferred_element_type=jnp.float32,
-    )
+    return real_product(a, jnp.concatenate([b, turned_rows], axis=0))
 
 
 def adjoint(a):
@@ -60,48 +67,55 @@
     def along_rows(v, k):
         return jnp.broadcast_to(v[k : k + 1], shape)
 
+    zero = jnp.zeros(shape, jnp.float32)
     for p in range(count):
         panel = groups[p]
         turned = times_i(panel)
         br = [along_lanes(panel, p * B + j) for j in range(B)]
         bi = [along_lanes(panel, H + p * B + j) for j in range(B)]
+        sr = zero
+        si = zero
         for k in range(B):
             own = row == k
+            mr = jnp.where(own, 0.0, br[k])
+            mi = jnp.where(own, 0.0, bi[k])
             qr = along_rows(br[k], k)
             qi = along_rows(bi[k], k)
             s = 1.0 / (qr * qr + qi * qi)
-            vr = qr * s
-            vi = -qi * s
-            mr = jnp.where(own, 0.0, br[k])
-            mi = jnp.where(own, 0.0, bi[k])
+            ur = (mr * qr + mi * qi) * s
+            ui = (mi * qr - mr * qi) * s
+            sr = jnp.where(own, qr * s, sr)
+            si = jnp.where(own, -qi * s, si)
+            for j in range(k + 1, B):
+                yr = along_rows(br[j], k)
+                yi = along_rows(bi[j], k)
+                br[j] = br[j] - (ur * yr - ui * yi)
+                bi[j] = bi[j] - (ur * yi + ui * yr)
             here = column == p * B + k
             panel = jnp.where(here, jnp.where(own & (lane < H), 1.0, 0.0), panel)
             turned = jnp.where(here, jnp.where(own & (lane >= H), 1.0, 0.0), turned)
             y = along_rows(panel, k)
             ty = along_rows(turned, k)
-            r = y * vr + ty * vi
-            tr = ty * vr - y * vi
-            panel = jnp.where(own, r, panel - (mr * r + mi * tr))
-            turned = jnp.where(own, tr, turned - (mr * tr - mi * r))
-            for j in range(k + 1, B):
-                yr = along_rows(br[j], k)
-                yi = along_rows(bi[j], k)
-                rr = yr * vr - yi * vi
-                ri = yr * vi + yi * vr
-                br[j] = jnp.where(own, rr, br[j] - (mr * rr - mi * ri))
-                bi[j] = jnp.where(own, ri, bi[j] - (mr * ri + mi * rr))
+            panel = panel - (ur * y + ui * ty)
+            turned = turned - (ur * ty - ui * y)
+        panel, turned = sr * panel + si * turned, sr * turned - si * panel
+        old = list(groups)
         groups[p] = panel
         inside = (column >= p * B) & (column < (p + 1) * B)
-        rr = [along_rows(panel, j) for j in range(B)]
-        ri = [along_rows(turned, j) for j in range(B)]
-        for t in range(1, count):
-            g = (p + t) % count
-            old = groups[g]
-            new = jnp.where(inside, 0.0, old)
-            for j in range(B):
-                new = new - (
-                    along_lanes(old, p * B + j) * rr[j] + along_lanes(old, H + p * B + j) * ri[j]
-                )
+        spread = [zero] * p + [panel] + [zero] * (count - 1) + [turned] + [zero] * (count - 1 - p)
+        change = real_product(jnp.concatenate(old, axis=0), jnp.concatenate(spread, axis=0))
+        for g in range(count):
+            if g == p:
+                continue
+            new = jnp.where(inside, 0.0, old[g])
+            if g == p + 1:
+                for j in range(B):
+                    new = new - (
+                        along_lanes(old[g], p * B + j) * along_rows(panel, j)
+                        + along_lanes(old[g], H + p * B + j) * along_rows(turned, j)
+                    )
+            else:
+                new = new - change[g * B : (g + 1) * B]
             groups[g] = new
     return jnp.concatenate(groups, axis=0)
 
@@ -132,6 +146,17 @@
 def kernel(
     energy_count,
     partitions,
+    steps_hbm,
+    emission_hbm,
+    absorption_hbm,
+    lesser_hbm,
+    greater_hbm,
+    ham_hbm,
+    coupling_hbm,
+    lead_hbm,
+    green_ref,
+    in_ref,
+    out_ref,
     steps_ref,
     emission_ref,
     absorption_ref,
@@ -140,9 +165,6 @@
     ham_ref,
     coupling_ref,
     lead_ref,
-    green_ref,
-    in_ref,
-    out_ref,
     own_ref,
     window_ref,
     received,
@@ -171,7 +193,25 @@
     occ_recv,
     dom_send,
     dom_recv,
+    fetch_sems,
 ):
+    fetches = [
+        pltpu.make_async_copy(src, dst, fetch_sems.at[number])
+        for number, (src, dst) in enumerate(
+            (
+                (lesser_hbm, lesser_ref),
+                (greater_hbm, greater_ref),
+                (coupling_hbm, coupling_ref),
+                (lead_hbm, lead_ref),
+                (steps_hbm, steps_ref),
+                (emission_hbm, emission_ref),
+                (absorption_hbm, absorption_ref),
+                (ham_hbm, ham_ref),
+            )
+        )
+    ]
+    for fetch in fetches:
+        fetch.start()
     energy = lax.axis_index("energy")
     dom = lax.axis_index("dom")
     half = (2 * dom >= partitions).astype(jnp.int32)
@@ -203,6 +243,8 @@
         def _():
             pl.semaphore_signal(barrier, inc=1, device_id={"dom": dom + o}, device_id_type=MESH)
 
+    fetches[0].wait()
+    fetches[1].wait()
     own_ref[0:2] = lesser_ref[0]
     own_ref[2:4] = greater_ref[0]
     own_ref[4:8] = jnp.zeros((4, N), jnp.float32)
@@ -229,6 +271,8 @@
         def _():
             window_ref[number] = jnp.zeros((8, N), jnp.float32)
 
+    for fetch in fetches[2:]:
+        fetch.wait()
     link = jnp.concatenate([coupling_ref[1, 0], coupling_ref[1, 1]], axis=1)
     link_adjoint = adjoint(link)
     outer = jnp.concatenate([coupling_ref[0, 0], coupling_ref[0, 1]], axis=1)
@@ -489,7 +533,8 @@
     absorption_strength,
 ):
     whole = pl.BlockSpec(memory_space=pltpu.VMEM)
-    scalars = pl.BlockSpec(memory_space=pltpu.SMEM)
+    outside = pl.BlockSpec(memory_space=pltpu.HBM)
+    mode_scalars = pltpu.SMEM((MODES,), jnp.float32)
     matrix = pltpu.VMEM((N, 2 * N), jnp.float32)
     pair = pltpu.VMEM((2, N, 2 * N), jnp.float32)
     reach = 2 * SMAX
@@ -500,9 +545,17 @@
             jax.ShapeDtypeStruct((1, 2, N), jnp.float32),
             jax.ShapeDtypeStruct((1, 2, N), jnp.float32),
         ),
-        in_specs=[scalars] * 3 + [whole] * 5,
+        in_specs=[outside] * 8,
         out_specs=(whole,) * 3,
         scratch_shapes=[
+            pltpu.SMEM((MODES,), jnp.int32),
+            mode_scalars,
+            mode_scalars,
+            pltpu.VMEM(lesser_occupancy.shape, jnp.float32),
+            pltpu.VMEM(greater_occupancy.shape, jnp.float32),
+            pltpu.VMEM(hamiltonian.shape, jnp.float32),
+            pltpu.VMEM(couplings.shape, jnp.float32),
+            pltpu.VMEM(right_lead.shape, jnp.float32),
             pltpu.VMEM((8, N), jnp.float32),
             pltpu.VMEM((reach, 8, N), jnp.float32),
             pair,
@@ -514,6 +567,7 @@
             pltpu.SemaphoreType.DMA((reach,)),
             pltpu.SemaphoreType.DMA((2,)),
             pltpu.SemaphoreType.DMA((2,)),
+            pltpu.SemaphoreType.DMA((8,)),
         ],
         compiler_params=pltpu.CompilerParams(
             collective_id=0, has_side_effects=True, vmem_limit_bytes=40 * 2**20

time: 65.3 us -> 59.9 us (0.917)
  Pallas kernels: 56.4 us -> 51 us
    pallas_call x1, Pallas kernels: 56.4 us -> 51 us  [local(): pl.pallas_call(functools.partial(kernel, lax.axis_size('energy'), lax.axi...]
where the time goes in v2:
time: 59.9 us; the launch traced here: 59.6 us
  Pallas kernels  51 us (85%)
  local copies, waits for them, and re-layouts  7.95 us (13%)
  between operations  0.66 us (1%)
    pallas_call x1, Pallas kernels, local(): pl.pallas_call(functools.partial(kernel, lax.axis_size('energy'), lax.axi...  51 us
    unnamed x19, local copies, waits for them, and re-layouts  7.95 us

profile of v2, /device:TPU:0, one launch (start us, length us, event | category | flops | bytes accessed | tf_op | source)
XLA Modules:
  0.0 59.6 jit_solution(12836567685479445946)
XLA Ops:
  0.6 0.0 copy-start
  0.6 0.9 %copy-done = f32[2,2,128,128]{3,2,1,0:T(8,128)S(1)} copy-done((f32[2,2,128,128]{3,2,1,0:T(8,128)S(1)}, f32[2,2,128,128]{3,2,1,0:T(8,128)}, u32[]{:S(2)}) %copy-start) | copy-done | bytes 262168
  1.6 0.0 copy-start.1
  1.6 0.9 %copy-done.1 = f32[2,2,128,128]{3,2,1,0:T(8,128)S(1)} copy-done((f32[2,2,128,128]{3,2,1,0:T(8,128)S(1)}, f32[2,2,128,128]{3,2,1,0:T(8,128)}, u32[]{:S(2)}) %copy-start.1) | copy-done | bytes 262168
  2.5 0.0 copy-start.2
  2.5 0.9 %copy-done.2 = f32[2,128,128]{2,1,0:T(8,128)S(1)} copy-done((f32[2,128,128]{2,1,0:T(8,128)S(1)}, f32[2,128,128]{2,1,0:T(8,128)}, u32[]{:S(2)}) %copy-start.2) | copy-done | bytes 131096
  3.4 0.0 copy-start.3
  3.4 0.7 %copy-done.3 = f32[1,2,128]{2,1,0:T(2,128)S(1)} copy-done((f32[1,2,128]{2,1,0:T(2,128)S(1)}, f32[1,2,128]{2,1,0:T(2,128)}, u32[]{:S(2)}) %copy-start.3) | copy-done | bytes 1048
  4.1 0.0 copy-start.4
  4.1 0.7 %copy-done.4 = f32[1,2,128]{2,1,0:T(2,128)S(1)} copy-done((f32[1,2,128]{2,1,0:T(2,128)S(1)}, f32[1,2,128]{2,1,0:T(2,128)}, u32[]{:S(2)}) %copy-start.4) | copy-done | bytes 1048
  4.8 0.0 copy-start.5
  4.8 0.7 %copy-done.5 = s32[6]{0:T(128)S(1)} copy-done((s32[6]{0:T(128)S(1)}, s32[6]{0:T(128)}, u32[]{:S(2)}) %copy-start.5) | copy-done | bytes 48
  5.5 0.0 copy-start.6
  5.5 0.7 %copy-done.6 = f32[6]{0:T(128)S(1)} copy-done((f32[6]{0:T(128)S(1)}, f32[6]{0:T(128)}, u32[]{:S(2)}) %copy-start.6) | copy-done | bytes 48
  6.1 0.0 copy-start.7
  6.1 0.7 %copy-done.7 = f32[6]{0:T(128)S(1)} copy-done((f32[6]{0:T(128)S(1)}, f32[6]{0:T(128)}, u32[]{:S(2)}) %copy-start.7) | copy-done | bytes 48
  6.8 51.0 %shard_map.103 = (f32[1,2,2,128,128]{4,3,2,1,0:T(8,128)S(1)}, f32[1,2,128]{2,1,0:T(2,128)S(1)}, f32[1,2,128]{2,1,0:T(2,128)S(1)}) custom-call(s32[6]{0:T(128)S(1)} %copy-done.5, f32[6]{0:T(128)S(1)} %copy-done.6, f32[6]{0:T(128)S(1)} %copy-done.7, f32[1,2,128]{2,1,0:T(2,128)S(1)} %copy-done.3, f32[1,2,128]{2,1,0:T(2,128)S(1)} %copy-done.4, ...), custom_call_target="tpu_custom_call" | custom-call | tf_op jit(solution)/shard_map/pallas_call | solution.py:541
  57.8 0.7 %copy.14 = f32[1,2,2,128,128]{4,3,2,1,0:T(8,128)} copy(f32[1,2,2,128,128]{4,3,2,1,0:T(8,128)S(1)} %get-tuple-element.6) | data formatting | bytes 524288
  58.5 0.6 copy.15
  59.0 0.6 copy.16
Async XLA Ops:
  0.6 1.0 %copy-start = (f32[2,2,128,128]{3,2,1,0:T(8,128)S(1)}, f32[2,2,128,128]{3,2,1,0:T(8,128)}, u32[]{:S(2)}) copy-start(f32[2,2,128,128]{3,2,1,0:T(8,128)} %ham_hbm.1) | copy-start | bytes 786436
  1.6 0.9 %copy-start.1 = (f32[2,2,128,128]{3,2,1,0:T(8,128)S(1)}, f32[2,2,128,128]{3,2,1,0:T(8,128)}, u32[]{:S(2)}) copy-start(f32[2,2,128,128]{3,2,1,0:T(8,128)} %coupling_hbm.1) | copy-start | bytes 786436
  2.5 0.9 %copy-start.2 = (f32[2,128,128]{2,1,0:T(8,128)S(1)}, f32[2,128,128]{2,1,0:T(8,128)}, u32[]{:S(2)}) copy-start(f32[2,128,128]{2,1,0:T(8,128)} %lead_hbm.1) | copy-start | bytes 393220
  3.4 0.7 %copy-start.3 = (f32[1,2,128]{2,1,0:T(2,128)S(1)}, f32[1,2,128]{2,1,0:T(2,128)}, u32[]{:S(2)}) copy-start(f32[1,2,128]{2,1,0:T(2,128)} %lesser_hbm.1) | copy-start | bytes 3076
  4.1 0.7 %copy-start.4 = (f32[1,2,128]{2,1,0:T(2,128)S(1)}, f32[1,2,128]{2,1,0:T(2,128)}, u32[]{:S(2)}) copy-start(f32[1,2,128]{2,1,0:T(2,128)} %greater_hbm.1) | copy-start | bytes 3076
  4.8 0.7 %copy-start.5 = (s32[6]{0:T(128)S(1)}, s32[6]{0:T(128)}, u32[]{:S(2)}) copy-start(s32[6]{0:T(128)} %steps_hbm.1) | copy-start | bytes 76
  5.5 0.7 %copy-start.6 = (f32[6]{0:T(128)S(1)}, f32[6]{0:T(128)}, u32[]{:S(2)}) copy-start(f32[6]{0:T(128)} %emission_hbm.1) | copy-start | bytes 76
  6.1 0.7 %copy-start.7 = (f32[6]{0:T(128)S(1)}, f32[6]{0:T(128)}, u32[]{:S(2)}) copy-start(f32[6]{0:T(128)} %absorption_hbm.1) | copy-start | bytes 76

commit v3 on v2

--- a/solution.py
+++ b/solution.py
@@ -570,7 +570,7 @@
             pltpu.SemaphoreType.DMA((8,)),
         ],
         compiler_params=pltpu.CompilerParams(
-            collective_id=0, has_side_effects=True, vmem_limit_bytes=40 * 2**20
+            collective_id=0, has_side_effects=True, vmem_limit_bytes=63 * 2**20 + 2**19
         ),
     )(
         phonon_steps,

time: 59.9 us -> 55.2 us (0.922)
  local copies, waits for them, and re-layouts: 7.95 us -> 2.91 us
    unnamed x19 -> x7, local copies, waits for them, and re-layouts: 7.95 us -> 2.91 us
where the time goes in v3:
time: 55.2 us; the launch traced here: 55.1 us
  Pallas kernels  51.5 us (93%)
  local copies, waits for them, and re-layouts  2.91 us (5%)
  between operations  0.65 us (1%)
    pallas_call x1, Pallas kernels, local(): pl.pallas_call(functools.partial(kernel, lax.axis_size('energy'), lax.axi...  51.5 us
    unnamed x7, local copies, waits for them, and re-layouts  2.91 us

profile of v3, /device:TPU:0, one launch (start us, length us, event | category | flops | bytes accessed | tf_op | source)
XLA Modules:
  0.0 55.1 jit_solution(15539206018553417752)
XLA Ops:
  0.6 51.5 %shard_map.103 = (f32[1,2,2,128,128]{4,3,2,1,0:T(8,128)}, f32[1,2,128]{2,1,0:T(2,128)}, f32[1,2,128]{2,1,0:T(2,128)}) custom-call(s32[6]{0:T(128)} %steps_hbm.1, f32[6]{0:T(128)} %emission_hbm.1, f32[6]{0:T(128)} %absorption_hbm.1, f32[1,2,128]{2,1,0:T(2,128)} %lesser_hbm.1, f32[1,2,128]{2,1,0:T(2,128)} %greater_hbm.1, f32[2,2,128,128]{3,2,1,0:T(8,128)} %ham_hbm.1, ...), custom_call_target="tpu_custom_call" | custom-call | tf_op jit(solution)/shard_map/pallas_call | solution.py:541
  52.2 0.0 copy-start.1
  52.2 1.7 %copy.14 = f32[1,2,2,128,128]{4,3,2,1,0:T(8,128)} copy(f32[1,2,2,128,128]{4,3,2,1,0:T(8,128)} %get-tuple-element.6) | data formatting | bytes 524288
  53.8 0.0 copy-done.1
  53.8 0.0 copy-start
  53.8 0.6 %copy.15 = f32[1,2,128]{2,1,0:T(2,128)} copy(f32[1,2,128]{2,1,0:T(2,128)S(1)} %copy-done.1) | data formatting | bytes 2048
  54.4 0.1 copy-done
  54.5 0.6 %copy.16 = f32[1,2,128]{2,1,0:T(2,128)} copy(f32[1,2,128]{2,1,0:T(2,128)S(1)} %copy-done) | data formatting | bytes 2048
Async XLA Ops:
  52.2 1.7 %copy-start.1 = (f32[1,2,128]{2,1,0:T(2,128)S(1)}, f32[1,2,128]{2,1,0:T(2,128)}, u32[]{:S(2)}) copy-start(f32[1,2,128]{2,1,0:T(2,128)} %get-tuple-element.7) | copy-start | bytes 3076
  53.8 0.7 %copy-start = (f32[1,2,128]{2,1,0:T(2,128)S(1)}, f32[1,2,128]{2,1,0:T(2,128)}, u32[]{:S(2)}) copy-start(f32[1,2,128]{2,1,0:T(2,128)} %get-tuple-element.8) | copy-start | bytes 3076
